TPU v7x, 512 devices: a whole 4x4x16 slice. The times are simulated.
512 devices in a mesh: head: 32 (over y, x, core), ctx: 16 (over z).
Axes of the slice: x: 4, y: 4, z: 16, core: 2. Of those that a mesh axis runs over, the one named last changes fastest.
Arguments:
- queries: bfloat16 [65536, 4096], P(('ctx', 'head')), may hold values from -30 to 30
- keys: bfloat16 [65536, 4096], P(('ctx', 'head')), may hold values from -6 to 6
- values: bfloat16 [65536, 4096], P(('ctx', 'head')), may hold values from -6 to 6
- pattern: int32 [512, 5], replicated, may hold values from 0 to 511, as said below
Outputs:
- attended: bfloat16 [65536, 4096], P(('ctx', 'head'))
Inputs may be any that keep to these rules, and one draw needn't show every extreme that they name: `pattern`: row a lists 5 different query blocks, none of them a. The entries of the 32 rows c * 32 to (c + 1) * 32 - 1 name the blocks d * 32 to (d + 1) * 32 - 1 exactly 10 times, for every c and d.
All inputs are finite; a program needn't handle non-finite values.
Results may differ from a plain program's by a relative error of at most 0.0075.
Values may be sent and summed in bfloat16 or wider, within the bound.
No kernel may reach another device: no remote copies, remote signals or barrier semaphores. Data moves between devices by JAX's collectives and lax.ppermute only.
A program may use at most 128 MiB of HBM per device.

v0:
```python
import jax
import jax.numpy as jnp
from jax import lax
from jax.sharding import PartitionSpec as P

HD = 128
BLOCK = 128
QPER = 5


def block_partial(query_part, key_part, value_part):
    count, length, width = query_part.shape
    heads_here = width // HD
    query_heads = query_part.reshape(count, length, heads_here, HD)
    key_heads = key_part.reshape(count, length, heads_here, HD)
    value_heads = value_part.reshape(count, length, heads_here, HD)
    scores = jnp.einsum(
        "nqhd,nkhd->nhqk", query_heads, key_heads, preferred_element_type=jnp.float32
    ) * HD ** (-0.5)
    peak = jnp.max(scores, axis=-1)
    expo = jnp.exp(scores - peak[..., None])
    total = jnp.sum(expo, axis=-1)
    weights = expo.astype(jnp.bfloat16)
    mixed = jnp.einsum("nhqk,nkhd->nqhd", weights, value_heads, preferred_element_type=jnp.float32)
    normed = (mixed / jnp.transpose(total, (0, 2, 1))[..., None]).astype(jnp.bfloat16)
    return (normed.reshape(count, length, width), peak + jnp.log(total))


def slot_tables(entries, target, blocks_here, capacity):
    count = entries.shape[0]
    hit = (entries // blocks_here == target).astype(jnp.int32)
    ranked = jnp.cumsum(hit) - 1
    chosen = hit[:, None] * (ranked[:, None] == jnp.arange(capacity)[None, :]).astype(jnp.int32)
    key_local = jnp.sum(chosen * (jnp.arange(count) // QPER)[:, None], axis=0)
    query_local = jnp.sum(chosen * (entries % blocks_here)[:, None], axis=0)
    filled = jnp.sum(chosen, axis=0)
    return (key_local, query_local, filled)


def body(queries, keys, values, pattern):
    query_rows, key_rows, value_rows = (
        lax.all_to_all(queries, "head", split_axis=1, concat_axis=0, tiled=True),
        lax.all_to_all(keys, "head", split_axis=1, concat_axis=0, tiled=True),
        lax.all_to_all(values, "head", split_axis=1, concat_axis=0, tiled=True),
    )
    length, width = query_rows.shape
    blocks_here = length // BLOCK
    heads_here = width // HD
    shards = lax.axis_size("ctx")
    position = lax.axis_index("ctx")
    capacity = blocks_here * QPER // shards
    slots = shards * capacity
    query_blocks = query_rows.reshape(blocks_here, BLOCK, width)
    key_blocks = key_rows.reshape(blocks_here, BLOCK, width)
    value_blocks = value_rows.reshape(blocks_here, BLOCK, width)
    mine = lax.dynamic_slice_in_dim(pattern, position * blocks_here, blocks_here, 0).reshape(-1)
    send_key, send_query, send_fill = jax.vmap(slot_tables, in_axes=(None, 0, None, None))(
        mine, jnp.arange(shards, dtype=jnp.int32), blocks_here, capacity
    )
    owner_key, owner_query, owner_fill = jax.vmap(slot_tables, in_axes=(0, None, None, None))(
        pattern.reshape(shards, -1), position, blocks_here, capacity
    )
    diag_out, diag_levels = block_partial(query_blocks, key_blocks, value_blocks)
    outgoing = jnp.take(query_blocks, owner_query, axis=0)
    fetched = lax.all_to_all(outgoing, "ctx", split_axis=0, concat_axis=0, tiled=True)
    flat_key = send_key.reshape(-1)
    part_out, part_levels = block_partial(
        fetched.reshape(slots, BLOCK, width),
        jnp.take(key_blocks, flat_key, axis=0),
        jnp.take(value_blocks, flat_key, axis=0),
    )
    part_out = part_out.reshape(shards, capacity, BLOCK, width)
    part_levels = part_levels.reshape(shards, capacity, heads_here, BLOCK)
    recv_out = lax.all_to_all(part_out, "ctx", split_axis=0, concat_axis=0, tiled=True)
    recv_levels = lax.all_to_all(part_levels, "ctx", split_axis=0, concat_axis=0, tiled=True)
    highest = lax.Precision.HIGHEST
    live = owner_fill > 0
    select = (
        (owner_query[..., None] == jnp.arange(blocks_here)[None, None, :]) & live[..., None]
    ).astype(jnp.float32)
    masked = jnp.where(live[:, :, None, None], recv_levels, -jnp.inf)
    candidate = jnp.where(select[:, :, :, None, None] > 0, masked[:, :, None], -jnp.inf)
    best = jnp.maximum(diag_levels, jnp.max(candidate, axis=(0, 1)))
    best_at = jnp.einsum("scb,bhq->schq", select, best, precision=highest)
    shares = jnp.exp(masked - best_at)
    diag_share = jnp.exp(diag_levels - best)
    denom = diag_share + jnp.einsum("scb,schq->bhq", select, shares, precision=highest)
    start = (
        diag_out.astype(jnp.float32).reshape(blocks_here, BLOCK, heads_here, HD)
        * jnp.transpose(diag_share, (0, 2, 1))[..., None]
    )
    weighted = (
        recv_out.astype(jnp.float32).reshape(shards, capacity, BLOCK, heads_here, HD)
        * jnp.transpose(shares, (0, 1, 3, 2))[..., None]
    )
    numer = start + jnp.einsum("scb,scqhd->bqhd", select, weighted, precision=highest)
    attended = (
        (numer / jnp.transpose(denom, (0, 2, 1))[..., None])
        .astype(jnp.bfloat16)
        .reshape(length, width)
    )
    return lax.all_to_all(attended, "head", split_axis=0, concat_axis=1, tiled=True)


def solution(mesh):
    in_specs = (P(("ctx", "head"), None), P(("ctx", "head"), None), P(("ctx", "head"), None), P())
    out_specs = P(("ctx", "head"), None)
    return jax.shard_map(body, mesh=mesh, in_specs=in_specs, out_specs=out_specs, check_vma=False)
```

profile of v0, /device:TPU:1, one launch (start us, length us, event | category | flops | bytes accessed | tf_op | source)
XLA Modules:
  0.0 645.6 jit_solution(12804778365043559937)
XLA Ops:
  0.0 1.7 copy.123
  1.7 1.3 copy.124
  3.0 10.5 %all-to-all-start = ((bf16[128,32,128]{2,0,1:T(8,128)(2,1)}), bf16[128,32,128]{2,0,1:T(8,128)(2,1)S(1)}, u32[]{:S(2)}, u32[]{:S(2)}) async-start(bf16[128,32,128]{2,0,1:T(8,128)(2,1)} %copy.124), calls=%async_computation | async-start | bytes 2097152 | tf_op jit(solution)/shard_map/all_to_all | solution.py:42
  13.5 0.1 copy.130
  13.7 0.2 reshape.355
  13.8 0.7 copy.125
  14.5 1.3 copy.126
  15.8 14.9 %all-to-all-done = bf16[128,32,128]{2,0,1:T(8,128)(2,1)S(1)} async-done(((bf16[128,32,128]{2,0,1:T(8,128)(2,1)}), bf16[128,32,128]{2,0,1:T(8,128)(2,1)S(1)}, u32[]{:S(2)}, u32[]{:S(2)}) %all-to-all-start) | async-done | bytes 1048608 | tf_op jit(solution)/shard_map/all_to_all | solution.py:42
  30.8 4.0 all-to-all-start.1
  34.8 0.6 reduce-window.14
  35.4 0.2 slice_reduce_fusion.1
  35.6 1.6 copy.127
  37.3 1.3 copy.128
  38.7 0.4 select_reduce_fusion.1
  39.1 13.0 %all-to-all-done.1 = bf16[128,32,128]{2,0,1:T(8,128)(2,1)S(1)} async-done(((bf16[128,32,128]{2,0,1:T(8,128)(2,1)}), bf16[128,32,128]{2,0,1:T(8,128)(2,1)S(1)}, u32[]{:S(2)}, u32[]{:S(2)}) %all-to-all-start.1) | async-done | bytes 1048608 | tf_op jit(solution)/shard_map/all_to_all | solution.py:43
  52.1 4.0 all-to-all-start.2
  56.3 7.7 %gather_fusion = bf16[160,128,128]{2,1,0:T(8,128)(2,1)} fusion(bf16[32,128,128]{2,1,0:T(8,128)(2,1)S(1)} %bitcast.97, s32[1024]{0:T(1024)S(1)} %pad_clamp_fusion.1), kind=kCustom, calls=%fused_computation.2 | custom fusion | bytes 10486400 | tf_op jit(solution)/shard_map/jit(_take)/gather | solution.py:64
  64.1 5.3 broadcast_select_fusion
  69.4 3.9 all-to-all-done.2
  73.3 13.2 %all-to-all-start.3 = ((bf16[16,10,128,128]{3,2,1,0:T(8,128)(2,1)}), bf16[16,10,128,128]{3,2,1,0:T(8,128)(2,1)}, u32[]{:S(2)}, u32[]{:S(2)}) async-start(bf16[16,10,128,128]{3,2,1,0:T(8,128)(2,1)} %broadcast_select_fusion), calls=%async_computation.3 | async-start | bytes 10485760 | tf_op jit(solution)/shard_map/all_to_all | solution.py:65
  86.7 0.1 reshape.359
  86.8 0.6 reduce-window.16
  87.4 0.2 slice_reduce_fusion
  87.7 0.3 multiply_reduce_fusion.2
  88.2 7.7 %gather_fusion.1 = bf16[160,128,128]{2,1,0:T(8,128)(2,1)} fusion(bf16[32,128,128]{2,1,0:T(8,128)(2,1)S(1)} %bitcast.98, s32[1024]{0:T(1024)S(1)} %pad_clamp_fusion), kind=kCustom, calls=%fused_computation.clone | custom fusion | bytes 10486400 | tf_op jit(solution)/shard_map/jit(_take)/gather | solution.py:69
  95.9 7.7 %gather_fusion.2 = bf16[160,128,128]{2,1,0:T(8,128)(2,1)} fusion(bf16[32,128,128]{2,1,0:T(8,128)(2,1)S(1)} %bitcast.99, s32[1024]{0:T(1024)S(1)} %pad_clamp_fusion), kind=kCustom, calls=%fused_computation.1.clone | custom fusion | bytes 10486400 | tf_op jit(solution)/shard_map/jit(_take)/gather | solution.py:70
  103.7 209.6 %all-to-all-done.3 = bf16[16,10,128,128]{3,2,1,0:T(8,128)(2,1)} async-done(((bf16[16,10,128,128]{3,2,1,0:T(8,128)(2,1)}), bf16[16,10,128,128]{3,2,1,0:T(8,128)(2,1)}, u32[]{:S(2)}, u32[]{:S(2)}) %all-to-all-start.3) | async-done | bytes 5242912 | tf_op jit(solution)/shard_map/all_to_all | solution.py:65
  313.3 11.9 %multiply_reduce_fusion = (f32[160,128]{1,0:T(8,128)S(1)}, f32[160,128,128]{1,2,0:T(8,128)}) fusion(bf16[160,128,128]{2,1,0:T(8,128)(2,1)} %bitcast.12, bf16[160,128,128]{2,1,0:T(8,128)(2,1)} %gather_fusion.1, pred[160]{0:T(512)(128)(4,1)S(1)} %compare_and_fusion.1), kind=kOutput, calls=%fused_computation.9 | convolution fusion | flops 678932480 | bytes 21053600 | tf_op jit(solution)/shard_map/nqhd,nkhd->nhqk/dot_general | solution.py:17
  325.1 6.6 %fusion.4 = f32[160,128]{1,0:T(8,128)S(1)} fusion(f32[160,128,128]{1,2,0:T(8,128)} %get-tuple-element.9, f32[160,128]{1,0:T(8,128)S(1)} %get-tuple-element.8), kind=kLoop, calls=%fused_computation.11 | loop fusion | flops 7843840 | bytes 10649600 | tf_op jit(solution)/shard_map/reduce_sum | solution.py:22
  331.7 0.7 log_add_fusion
  332.4 11.5 %all-to-all-start.4 = ((f32[16,10,1,128]{3,2,1,0:T(1,128)}), f32[16,10,1,128]{3,2,1,0:T(1,128)S(1)}, u32[]{:S(2)}, u32[]{:S(2)}) async-start(f32[16,10,1,128]{3,2,1,0:T(1,128)} %bitcast.13), calls=%async_computation.4 | async-start | bytes 163840 | tf_op jit(solution)/shard_map/all_to_all | solution.py:75
  343.8 11.4 %fusion = bf16[160,1,128,128]{3,2,0,1:T(8,128)(2,1)} fusion(f32[160,128]{1,0:T(8,128)S(1)} %fusion.4, f32[160,128,128]{1,2,0:T(8,128)} %get-tuple-element.9, f32[160,128]{1,0:T(8,128)S(1)} %get-tuple-element.8, bf16[160,128,128]{2,1,0:T(8,128)(2,1)} %gather_fusion.2, pred[160]{0:T(512)(128)(4,1)S(1)} %compare_and_fusion.1), kind=kOutput, calls=%fused_computation.4 | convolution fusion | flops 686817280 | bytes 21135520 | tf_op jit(solution)/shard_map/nhqk,nkhd->nqhd/dot_general | solution.py:24
  355.3 7.9 %copy.145 = bf16[16,10,128,128]{3,2,1,0:T(8,128)(2,1)} copy(bf16[16,10,128,128]{2,3,1,0:T(8,128)(2,1)} %bitcast.101) | data formatting | bytes 10485760 | tf_op jit(solution)/shard_map/reshape;reshape | solution.py:72
  363.2 11.6 %all-to-all-start.5 = ((bf16[16,10,128,128]{3,2,1,0:T(8,128)(2,1)}), bf16[16,10,128,128]{3,2,1,0:T(8,128)(2,1)}, u32[]{:S(2)}, u32[]{:S(2)}) async-start(bf16[16,10,128,128]{3,2,1,0:T(8,128)(2,1)} %copy.145), calls=%async_computation.5 | async-start | bytes 10485760 | tf_op jit(solution)/shard_map/all_to_all | solution.py:74
  374.8 0.1 convert_compare_fusion
  374.9 0.9 multiply_reduce_fusion.1
  375.8 1.3 copy-done
  377.1 0.4 fusion.24
  377.6 1.0 select_reduce_fusion
  378.6 0.3 fusion.31
  379.0 0.3 fusion.32
  379.3 222.2 %all-to-all-done.5 = bf16[16,10,128,128]{3,2,1,0:T(8,128)(2,1)} async-done(((bf16[16,10,128,128]{3,2,1,0:T(8,128)(2,1)}), bf16[16,10,128,128]{3,2,1,0:T(8,128)(2,1)}, u32[]{:S(2)}, u32[]{:S(2)}) %all-to-all-start.5) | async-done | bytes 5242912 | tf_op jit(solution)/shard_map/all_to_all | solution.py:74
  601.5 6.5 %convert_multiply_fusion = f32[16,10,128,128]{3,2,1,0:T(8,128)S(1)} fusion(bf16[16,10,128,128]{3,2,1,0:T(8,128)(2,1)} %all-to-all-done.5, f32[16,10,128]{2,1,0:T(8,128)S(1)} %copy.146), kind=kLoop, calls=%fused_computation.7 | loop fusion | flops 5242880 | bytes 15810560 | tf_op jit(solution)/shard_map/mul | solution.py:93
  608.1 9.9 %fusion.26 = f32[32,128,128]{2,0,1:T(8,128)S(1)} fusion(f32[16,10,128,128]{3,2,1,0:T(8,128)S(1)} %convert_multiply_fusion, s32[16,10]{0,1:T(8,128)S(1)} %get-tuple-element.7, pred[16,10]{0,1:T(8,128)(4,1)S(1)} %broadcast_compare_fusion), kind=kOutput, calls=%fused_computation.34 | convolution fusion | flops 1006643200 | bytes 12583712 | tf_op jit(solution)/shard_map/scb,scqhd->bqhd/dot_general | solution.py:96
  618.0 3.1 fusion.18
  621.1 22.2 %all_to_all.79 = bf16[32,128,128]{2,1,0:T(8,128)(2,1)S(1)} all-to-all(bf16[32,128,128]{2,1,0:T(8,128)(2,1)S(1)} %fusion.18), channel_id=1, replica_groups=mesh['head'=32,'ctx'=16] {'head'}, dimensions={0} | all-to-all | bytes 2097152 | tf_op jit(solution)/shard_map/all_to_all | solution.py:102
  643.2 0.7 copy.149
  643.9 1.3 copy.150
  (41 shorter events, 1.1 us)
Async XLA Ops:
  0.0 13.5 %copy-start.3 = (s32[512,5]{0,1:T(8,128)S(1)}, s32[512,5]{0,1:T(8,128)}, u32[]{:S(2)}) copy-start(s32[512,5]{0,1:T(8,128)} %param.9) | copy-start | bytes 30724
  0.0 13.8 %copy-start.2 = (bf16[128,4096]{1,0:T(8,128)(2,1)S(1)}, bf16[128,4096]{1,0:T(8,128)(2,1)}, u32[]{:S(2)}) copy-start(bf16[128,4096]{1,0:T(8,128)(2,1)} %param.7) | copy-start | bytes 3145732
  3.0 27.8 %all-to-all-start = ((bf16[128,32,128]{2,0,1:T(8,128)(2,1)}), bf16[128,32,128]{2,0,1:T(8,128)(2,1)S(1)}, u32[]{:S(2)}, u32[]{:S(2)}) async-start(bf16[128,32,128]{2,0,1:T(8,128)(2,1)} %copy.124), calls=%async_computation | async-start | bytes 2097152 | tf_op jit(solution)/shard_map/all_to_all | solution.py:42
  30.8 21.3 %all-to-all-start.1 = ((bf16[128,32,128]{2,0,1:T(8,128)(2,1)}), bf16[128,32,128]{2,0,1:T(8,128)(2,1)S(1)}, u32[]{:S(2)}, u32[]{:S(2)}) async-start(bf16[128,32,128]{2,0,1:T(8,128)(2,1)} %copy.126), calls=%async_computation.1 | async-start | bytes 2097152 | tf_op jit(solution)/shard_map/all_to_all | solution.py:43
  52.1 21.3 %all-to-all-start.2 = ((bf16[128,32,128]{2,0,1:T(8,128)(2,1)}), bf16[128,32,128]{2,0,1:T(8,128)(2,1)S(1)}, u32[]{:S(2)}, u32[]{:S(2)}) async-start(bf16[128,32,128]{2,0,1:T(8,128)(2,1)} %copy.128), calls=%async_computation.2 | async-start | bytes 2097152 | tf_op jit(solution)/shard_map/all_to_all | solution.py:44
  73.3 239.9 %all-to-all-start.3 = ((bf16[16,10,128,128]{3,2,1,0:T(8,128)(2,1)}), bf16[16,10,128,128]{3,2,1,0:T(8,128)(2,1)}, u32[]{:S(2)}, u32[]{:S(2)}) async-start(bf16[16,10,128,128]{3,2,1,0:T(8,128)(2,1)} %broadcast_select_fusion), calls=%async_computation.3 | async-start | bytes 10485760 | tf_op jit(solution)/shard_map/all_to_all | solution.py:65
  332.4 30.8 %all-to-all-start.4 = ((f32[16,10,1,128]{3,2,1,0:T(1,128)}), f32[16,10,1,128]{3,2,1,0:T(1,128)S(1)}, u32[]{:S(2)}, u32[]{:S(2)}) async-start(f32[16,10,1,128]{3,2,1,0:T(1,128)} %bitcast.13), calls=%async_computation.4 | async-start | bytes 163840 | tf_op jit(solution)/shard_map/all_to_all | solution.py:75
  363.2 238.3 %all-to-all-start.5 = ((bf16[16,10,128,128]{3,2,1,0:T(8,128)(2,1)}), bf16[16,10,128,128]{3,2,1,0:T(8,128)(2,1)}, u32[]{:S(2)}, u32[]{:S(2)}) async-start(bf16[16,10,128,128]{3,2,1,0:T(8,128)(2,1)} %copy.145), calls=%async_computation.5 | async-start | bytes 10485760 | tf_op jit(solution)/shard_map/all_to_all | solution.py:74
  375.8 1.3 copy-start
  608.0 9.9 %copy-start.1 = (f32[32,128,128]{1,2,0:T(8,128)S(1)}, f32[32,128,128]{1,2,0:T(8,128)}, u32[]{:S(2)}) copy-start(f32[32,128,128]{1,2,0:T(8,128)} %copy-done) | copy-start | bytes 6291460
where the time goes:
time: 652 us; the launch traced here: 646 us
  waiting for transfers between devices  464 us (71%)
  starting transfers between devices  54.6 us (8%)
  local copies, waits for them, and re-layouts  43.7 us (7%)
  matrix products  37.7 us (6%)
  other arithmetic  22.9 us (4%)
  blocking collectives  22.2 us (3%)
    all_to_all x1, waiting for transfers between devices, body(): lax.all_to_all(part_out, 'ctx', split_axis=0, concat_axis=0, tiled=True)  222 us
    all_to_all x1, waiting for transfers between devices, body(): lax.all_to_all(outgoing, 'ctx', split_axis=0, concat_axis=0, tiled=True)  210 us
    all_to_all x1, blocking collectives, body(): lax.all_to_all(attended, 'head', split_axis=0, concat_axis=1, tiled=True)  22.2 us
    all_to_all x1, waiting for transfers between devices, body(): lax.all_to_all(queries, 'head', split_axis=1, concat_axis=0, tiled=True)  14.9 us
    dot_general x2, matrix products, block_partial(): jnp.einsum('nhqk,nkhd->nqhd', weights, value_heads, preferred_element_typ...  14.5 us
    all_to_all x1, starting transfers between devices, body(): lax.all_to_all(outgoing, 'ctx', split_axis=0, concat_axis=0, tiled=True)  13.2 us
  transfers between devices with their start and end apart: 6, of which 5 were waited for; matrix products, arithmetic and copies ran while one was open for 9% of the time, Pallas kernels for 0%

commit v1 on v0

v1 whole, which is shorter than its diff:
```python
import functools

import jax
import jax.numpy as jnp
import numpy as np
from jax import lax
from jax.experimental import pallas as pl
from jax.experimental.pallas import tpu as pltpu
from jax.sharding import Mesh, PartitionSpec as P

HD = 128
BLOCK = 128
QPER = 5
AXES = ("yh", "yl", "xh", "xl", "core")
SPLIT = "yh"
GROUP = tuple(a for a in AXES if a != SPLIT)
OWN = 32
GANG = 8
ROOM = 168
CHUNKS = 384
DEPTH = 4
SCALE = float(np.log2(np.e)) * HD**-0.5


def list_kernel(code, mine, slots, bases, metas, count, filled):
    entries = code.shape[0]

    def start(q, carry):
        filled[q] = 1
        slots[q * ROOM] = mine[q]
        return carry

    lax.fori_loop(0, OWN, start, 0)
    filled[OWN] = 0

    def place(a, carry):
        key = mine[OWN + a]
        for j in range(QPER):
            q = code[a * QPER + j]
            at = filled[q]
            slots[q * ROOM + at] = key
            filled[q] = at + 1
        return carry

    lax.fori_loop(0, entries // QPER, place, 0)

    def cut(q, total):
        have = filled[q]
        gangs = (have + GANG - 1) // GANG

        def pad(i, carry):
            slots[q * ROOM + i] = mine[q]
            return carry

        lax.fori_loop(have, gangs * GANG, pad, 0)

        def gang(g, carry):
            left = jnp.minimum(have - g * GANG, GANG)
            bases[total + g] = q * ROOM + g * GANG
            metas[total + g] = ((q * 16 + left) * 2 + (g == 0).astype(jnp.int32)) * 2 + (
                g == gangs - 1
            ).astype(jnp.int32)
            return carry

        lax.fori_loop(0, gangs, gang, 0)
        return total + gangs

    count[0] = lax.fori_loop(0, OWN, cut, 0)


def pair_lists(code, mine):
    smem = pl.BlockSpec(memory_space=pltpu.SMEM)
    return pl.pallas_call(
        list_kernel,
        in_specs=[smem, smem],
        out_specs=[smem] * 4,
        out_shape=[
            jax.ShapeDtypeStruct((OWN * ROOM + code.shape[0],), jnp.int32),
            jax.ShapeDtypeStruct((CHUNKS,), jnp.int32),
            jax.ShapeDtypeStruct((CHUNKS,), jnp.int32),
            jax.ShapeDtypeStruct((8,), jnp.int32),
        ],
        scratch_shapes=[pltpu.SMEM((OWN + 1,), jnp.int32)],
        cost_estimate=pl.CostEstimate(flops=0, bytes_accessed=60_000_000, transcendentals=0),
    )(code, mine)


def attend_kernel(slots, bases, metas, count, q, k, vt, o, kbuf, vbuf, acc, peak, total, sem):
    gangs = count[0]
    acc[...] = jnp.zeros_like(acc)
    total[...] = jnp.zeros_like(total)
    peak[...] = jnp.zeros_like(peak)

    def copies(t):
        at = lax.rem(t, DEPTH)
        base = bases[t]
        made = []
        for j in range(GANG):
            key = slots[base + j]
            part = pl.ds(j * BLOCK, BLOCK)
            made.append(pltpu.make_async_copy(k.at[key], kbuf.at[at, part], sem.at[at, 0, j]))
            made.append(pltpu.make_async_copy(vt.at[key], vbuf.at[at, :, part], sem.at[at, 1, j]))
        return made

    def fetch(t):
        @pl.when(t < gangs)
        def _():
            for copy in copies(t):
                copy.start()

    for t in range(DEPTH - 1):
        fetch(t)

    def step(t, carry):
        fetch(t + DEPTH - 1)
        for copy in copies(t):
            copy.wait()
        at = lax.rem(t, DEPTH)
        meta = metas[t]
        last = lax.rem(meta, 2)
        first = lax.rem(meta // 2, 2)
        left = lax.rem(meta // 4, 16)
        mine = meta // 64
        scores = lax.dot_general(
            kbuf[at], q[mine], (((1,), (1,)), ((), ())), preferred_element_type=jnp.float32
        )
        row = lax.broadcasted_iota(jnp.int32, scores.shape, 0)
        scores = jnp.where(row < left * BLOCK, scores * SCALE, -1e30)
        old = jnp.where(first == 1, jnp.full((1, HD), -1e30, jnp.float32), peak[0:1])
        new = jnp.maximum(old, jnp.max(scores, axis=0, keepdims=True))
        expo = jnp.exp2(scores - new)
        keep = jnp.exp2(old - new)
        total_new = total[0:1] * keep + jnp.sum(expo, axis=0, keepdims=True)
        mixed = jnp.dot(vbuf[at], expo.astype(jnp.bfloat16), preferred_element_type=jnp.float32)
        acc_new = acc[...] * keep + mixed
        peak[0:1] = new
        total[0:1] = total_new
        acc[...] = acc_new

        @pl.when(last == 1)
        def _():
            o[mine] = (acc_new / total_new).T.astype(jnp.bfloat16)

        return carry

    lax.fori_loop(0, gangs, step, 0)


def attend(lists, q, k, vt):
    vmem = pl.BlockSpec((OWN, BLOCK, HD), lambda i, *_: (0, 0, 0))
    anywhere = pl.BlockSpec(memory_space=pl.ANY)
    return pl.pallas_call(
        attend_kernel,
        grid_spec=pltpu.PrefetchScalarGridSpec(
            num_scalar_prefetch=4,
            grid=(1,),
            in_specs=[vmem, anywhere, anywhere],
            out_specs=vmem,
            scratch_shapes=[
                pltpu.VMEM((DEPTH, GANG * BLOCK, HD), jnp.bfloat16),
                pltpu.VMEM((DEPTH, HD, GANG * BLOCK), jnp.bfloat16),
                pltpu.VMEM((HD, BLOCK), jnp.float32),
                pltpu.VMEM((8, BLOCK), jnp.float32),
                pltpu.VMEM((8, BLOCK), jnp.float32),
                pltpu.SemaphoreType.DMA((DEPTH, 2, GANG)),
            ],
        ),
        out_shape=jax.ShapeDtypeStruct((OWN, BLOCK, HD), jnp.bfloat16),
        compiler_params=pltpu.CompilerParams(vmem_limit_bytes=50 << 20),
        cost_estimate=pl.CostEstimate(
            flops=200 * 4 * BLOCK**3, bytes_accessed=20 << 20, transcendentals=200 * BLOCK**2
        ),
    )(*lists, q, k, vt)


def place_of(block):
    ctx, rest = block // 32, block % 32
    rank, split = jnp.zeros_like(block), jnp.zeros_like(block)
    for i, axis in enumerate(AXES):
        bit = (rest >> (len(AXES) - 1 - i)) & 1
        if axis == SPLIT:
            split = bit
        else:
            rank = rank * 2 + bit
    return rank, ctx * 2 + split


def body(queries, keys, values, pattern):
    exchange = ("ctx", SPLIT)

    def to_heads(x):
        return lax.all_to_all(x, exchange, split_axis=1, concat_axis=0, tiled=True)

    me = jnp.int32(0)
    for axis in GROUP:
        me = me * 2 + lax.axis_index(axis)
    rank, slot = place_of(pattern.reshape(-1))
    code = jnp.where(rank == me, slot, OWN)
    rank, slot = place_of(jnp.arange(pattern.shape[0], dtype=jnp.int32))
    mine = jnp.concatenate([me * OWN + jnp.arange(OWN, dtype=jnp.int32), rank * OWN + slot])

    key_rows = to_heads(keys)
    key_rows, values = lax.optimization_barrier((key_rows, values))
    key_all = lax.all_gather(key_rows.reshape(OWN, BLOCK, HD), GROUP, axis=0, tiled=True)
    value_rows = to_heads(values)
    value_rows, queries = lax.optimization_barrier((value_rows, queries))
    turned = jnp.swapaxes(value_rows.reshape(OWN, BLOCK, HD), 1, 2)
    value_all = lax.all_gather(turned, GROUP, axis=0, tiled=True)
    query_rows = to_heads(queries).reshape(OWN, BLOCK, HD)
    out = attend(pair_lists(code, mine), query_rows, key_all, value_all)
    return lax.all_to_all(
        out.reshape(OWN * BLOCK, HD), exchange, split_axis=0, concat_axis=1, tiled=True
    )


def solution(mesh):
    fine = Mesh(mesh.devices.reshape(2, 2, 2, 2, 2, 16), AXES + ("ctx",))
    rows = P(("ctx",) + AXES, None)
    return jax.shard_map(
        body, mesh=fine, in_specs=(rows, rows, rows, P()), out_specs=rows, check_vma=False
    )
```

time: 652 us -> 407 us (0.62)
  waiting for transfers between devices: 464 us -> 122 us
  blocking collectives: 22.2 us -> 200 us
  Pallas kernels: 0 us -> 49.5 us
  starting transfers between devices: 54.6 us -> 7.07 us
  matrix products: 37.7 us -> 0 us
  local copies, waits for them, and re-layouts: 43.7 us -> 13 us
  other arithmetic: 22.9 us -> 1.3 us
  between operations: 0.74 us -> 13.5 us
    all_to_all x6 -> x1, waiting for transfers between devices: 464 us -> 33.4 us  [to_heads(): return lax.all_to_all(x, exchange, split_axis=1, concat_axis=0, tiled=True)]
    all_to_all x1 -> x3, blocking collectives: 22.2 us -> 200 us  [the longest x2 132 us: to_heads(): return lax.all_to_all(x, exchange, split_axis=1, concat_axis=0, tiled=True)]
    all_gather x0 -> x2, waiting for transfers between devices: none -> 88.7 us  [the longest x1 88.7 us: body(): value_all = lax.all_gather(turned, GROUP, axis=0, tiled=True)]
    pallas_call x0 -> x2, Pallas kernels: none -> 49.5 us  [the longest x1 31.4 us: attend(): pl.pallas_call(attend_kernel, grid_spec=pltpu.PrefetchScalarGridSpec(num_...]
    all_to_all x6 -> x1, starting transfers between devices: 54.6 us -> 7.03 us  [to_heads(): return lax.all_to_all(x, exchange, split_axis=1, concat_axis=0, tiled=True)]
    dot_general x7 -> x0, matrix products: 37.7 us -> none  [the longest x2 14.5 us: block_partial(): jnp.einsum('nhqk,nkhd->nqhd', weights, value_heads, preferred_element_typ...]
    gather x3 -> x0, local copies, waits for them, and re-layouts: 23.2 us -> none  [the longest x1 7.75 us: body(): jnp.take(value_blocks, flat_key, axis=0)]
    another operation x5 -> x0, local copies, waits for them, and re-layouts: 8.06 us -> none  [the longest x1 7.86 us: body(): part_out = part_out.reshape(shards, capacity, BLOCK, width)]
  transfers between devices with their start and end apart: 6 -> 3, of which waited for: 5 -> 2; matrix products, arithmetic and copies ran while one was open for 9% -> 2% of each run, Pallas kernels for 0% -> 4%
where the time goes in v1:
time: 407 us
  blocking collectives  200 us (49%)
  waiting for transfers between devices  122 us (30%)
  Pallas kernels  49.5 us (12%)
  between operations  13.5 us (3%)
  local copies, waits for them, and re-layouts  13 us (3%)
  starting transfers between devices  7.07 us (2%)
    all_to_all x2, blocking collectives, to_heads(): return lax.all_to_all(x, exchange, split_axis=1, concat_axis=0, tiled=True)  132 us
    all_gather x1, waiting for transfers between devices, body(): value_all = lax.all_gather(turned, GROUP, axis=0, tiled=True)  88.7 us
    all_to_all x1, blocking collectives, body(): lax.all_to_all(out.reshape(OWN * BLOCK, HD), exchange, split_axis=0, conc...  68.5 us
    all_to_all x1, waiting for transfers between devices, to_heads(): return lax.all_to_all(x, exchange, split_axis=1, concat_axis=0, tiled=True)  33.4 us
    pallas_call x1, Pallas kernels, attend(): pl.pallas_call(attend_kernel, grid_spec=pltpu.PrefetchScalarGridSpec(num_...  31.4 us
    pallas_call x1, Pallas kernels, pair_lists(): pl.pallas_call(list_kernel, in_specs=[smem, smem], out_specs=[smem] * 4,...  18.1 us
  transfers between devices with their start and end apart: 3, of which 2 were waited for; matrix products, arithmetic and copies ran while one was open for 2% of the time, Pallas kernels for 4%

profile of v1, /device:TPU:1, one launch (start us, length us, event | category | flops | bytes accessed | tf_op | source)
XLA Modules:
  0.0 406.7 jit_solution(12114924975921147436)
XLA Ops:
  6.5 0.0 copy-start.4
  6.5 0.0 copy-start.5
  6.5 0.0 all-gather.3.cloned.1.call-start
  6.5 1.7 copy.31
  8.2 0.7 copy.32
  8.9 71.7 %all_to_all.70 = bf16[128,32,128]{2,0,1:T(8,128)(2,1)} all-to-all(bf16[128,32,128]{2,0,1:T(8,128)(2,1)S(1)} %copy.32), channel_id=1, replica_groups=mesh['yh'=2,'yl'=2,'xh'=2,'xl'=2,'core'=2,'ctx'=16] {'ctx','yh'}, dimensions={1} | all-to-all | bytes 2097152 | tf_op jit(solution)/shard_map/all_to_all | solution.py:192
  80.6 0.0 all-gather.3.cloned.1.call-update
  80.6 0.0 all-gather.5.cloned.1.call-start
  80.7 1.6 copy.33
  82.3 59.9 %all_to_all.71 = bf16[128,32,128]{0,2,1:T(8,128)(2,1)S(1)} all-to-all(bf16[128,32,128]{0,2,1:T(8,128)(2,1)S(1)} %bitcast.22), channel_id=1, replica_groups=mesh['yh'=2,'yl'=2,'xh'=2,'xl'=2,'core'=2,'ctx'=16] {'ctx','yh'}, dimensions={1} | all-to-all | bytes 2097152 | tf_op jit(solution)/shard_map/all_to_all | solution.py:192
  142.2 0.7 copy.34
  142.9 1.3 copy.37
  144.2 0.0 all-gather.5.cloned.1.call-update
  144.2 0.0 copy-done.4
  144.2 0.7 copy.35
  144.9 1.3 copy.36
  146.2 7.0 %all-to-all-start.2 = ((bf16[128,32,128]{2,0,1:T(8,128)(2,1)}), bf16[128,32,128]{2,0,1:T(8,128)(2,1)S(1)}, u32[]{:S(2)}, u32[]{:S(2)}) async-start(bf16[128,32,128]{2,0,1:T(8,128)(2,1)} %copy.36), calls=%async_computation.2 | async-start | bytes 2097152 | tf_op jit(solution)/shard_map/all_to_all | solution.py:192
  153.3 0.0 copy-done.5
  153.3 0.1 copy.30
  153.4 0.2 reshape.25
  153.7 0.7 pad_add_fusion.mine
  154.3 0.6 fusion.2.code
  155.0 18.1 %shard_map.46 = (s32[7936]{0:T(1024)}, s32[384]{0:T(512)}, s32[384]{0:T(512)}, s32[8]{0:T(128)}) custom-call(s32[2560]{0:T(1024)} %fusion.2.code, s32[544]{0:T(1024)} %pad_add_fusion.mine), custom_call_target="tpu_custom_call" | custom-call | bytes 60000000 | tf_op jit(solution)/shard_map/pallas_call | solution.py:73
  173.0 33.4 %all-to-all-done.2 = bf16[128,32,128]{2,0,1:T(8,128)(2,1)S(1)} async-done(((bf16[128,32,128]{2,0,1:T(8,128)(2,1)}), bf16[128,32,128]{2,0,1:T(8,128)(2,1)S(1)}, u32[]{:S(2)}, u32[]{:S(2)}) %all-to-all-start.2) | async-done | bytes 1048608 | tf_op jit(solution)/shard_map/all_to_all | solution.py:192
  206.4 0.0 all-gather.3.cloned.1.call-done.k
  206.4 88.7 %all-gather.5.cloned.1.call-done.vt = bf16[512,128,128]{2,1,0:T(8,128)(2,1)} async-done(((bf16[32,128,128]{2,1,0:T(8,128)(2,1)}), bf16[512,128,128]{2,1,0:T(8,128)(2,1)}) %all-gather.5.cloned.1.call-update) | async-done | bytes 16777232 | tf_op jit(solution)/shard_map/all_gather | solution.py:208
  295.1 0.0 copy-start
  295.1 0.8 copy-done
  295.9 0.0 copy-start.1
  295.9 0.7 copy-done.1
  296.6 0.0 copy-start.2
  296.6 0.7 copy-done.2
  297.2 0.0 copy-start.3
  297.2 0.7 copy-done.3
  297.9 31.4 %shard_map.47 = bf16[32,128,128]{2,1,0:T(8,128)(2,1)S(1)} custom-call(s32[7936]{0:T(1024)S(1)} %copy-done, s32[384]{0:T(512)S(1)} %copy-done.1, s32[384]{0:T(512)S(1)} %copy-done.2, s32[8]{0:T(128)S(1)} %copy-done.3, bf16[32,128,128]{2,1,0:T(8,128)(2,1)S(1)} %bitcast.15, bf16[512,128,128]{2,1,0:T(8,128)(2,1)} %all-gather.3.cloned.1.call-done.k, ...), custom_call_target="tpu_custom_call" | custom-call | flops 1677721600 | bytes 20971520 | tf_op jit(solution)/shard_map/pallas_call | solution.py:152
  329.4 68.5 %all_to_all.72 = bf16[32,128,128]{2,1,0:T(8,128)(2,1)S(1)} all-to-all(bf16[32,128,128]{2,1,0:T(8,128)(2,1)S(1)} %shard_map.47), channel_id=1, replica_groups=mesh['yh'=2,'yl'=2,'xh'=2,'xl'=2,'core'=2,'ctx'=16] {'ctx','yh'}, dimensions={0} | all-to-all | bytes 2097152 | tf_op jit(solution)/shard_map/all_to_all | solution.py:211
  397.9 0.7 copy.38
  398.5 1.3 copy.39
  (2 shorter events, 0.0 us)
Async XLA Ops:
  6.5 137.7 %copy-start.4 = (bf16[128,4096]{1,0:T(8,128)(2,1)S(1)}, bf16[128,4096]{1,0:T(8,128)(2,1)}, u32[]{:S(2)}) copy-start(bf16[128,4096]{1,0:T(8,128)(2,1)} %param.4) | copy-start | bytes 3145732
  6.5 146.7 %copy-start.5 = (s32[512,5]{0,1:T(8,128)S(1)}, s32[512,5]{0,1:T(8,128)}, u32[]{:S(2)}) copy-start(s32[512,5]{0,1:T(8,128)} %param.7) | copy-start | bytes 30724
  6.5 199.9 %all-gather.3.cloned.1.call-start = ((), (), s32[]{:S(2)}) async-start(), calls=%async_computation.4 | async-start | bytes 17825792 | tf_op jit(solution)/shard_map/all_gather | solution.py:204
  80.6 214.5 %all-gather.5.cloned.1.call-start = ((), (), s32[]{:S(2)}) async-start(), calls=%async_computation.5 | async-start | bytes 17825792 | tf_op jit(solution)/shard_map/all_gather | solution.py:208
  146.2 60.2 %all-to-all-start.2 = ((bf16[128,32,128]{2,0,1:T(8,128)(2,1)}), bf16[128,32,128]{2,0,1:T(8,128)(2,1)S(1)}, u32[]{:S(2)}, u32[]{:S(2)}) async-start(bf16[128,32,128]{2,0,1:T(8,128)(2,1)} %copy.36), calls=%async_computation.2 | async-start | bytes 2097152 | tf_op jit(solution)/shard_map/all_to_all | solution.py:192
  295.1 0.8 copy-start
  295.9 0.7 copy-start.1
  296.6 0.7 copy-start.2
  297.2 0.7 copy-start.3
Sparse Core Ops, SparseCore 0:
  80.8 111.5 all-gather.2
  194.5 100.5 all-gather.4

commit v2 on v1

v2 whole, which is shorter than its diff:
```python
import jax
import jax.numpy as jnp
import numpy as np
from jax import lax
from jax.experimental import pallas as pl
from jax.experimental.pallas import tpu as pltpu
from jax.sharding import Mesh, PartitionSpec as P

HD = 128
BLOCK = 128
QPER = 5
AXES = ("yh", "yl", "xh", "xl", "core")
SPLIT = "yh"
PAIR = "yl"
GROUP = ("xh", "xl", "core")
OWN = 32
GANG = 4
ROOM = 168
WIDTH = 8
GANGS = 680
DEPTH = 6
SCALE = float(np.log2(np.e)) * HD**-0.5
LOW = -1e30


def list_kernel(code, spot, theirs, ours, slots, filled):
    def start(q, carry):
        filled[q] = 0
        filled[OWN + q] = 1
        slots[(OWN + q) * ROOM] = spot[q]
        return carry

    lax.fori_loop(0, OWN, start, 0)
    filled[2 * OWN] = 0

    def place(a, carry):
        key = spot[OWN + a]
        for j in range(QPER):
            q = code[a * QPER + j]
            at = filled[q]
            slots[q * ROOM + at] = key
            filled[q] = at + 1
        return carry

    lax.fori_loop(0, code.shape[0] // QPER, place, 0)

    for side, plan in ((0, theirs), (1, ours)):

        def cut(q, total):
            row = side * OWN + q
            have = filled[row]
            gangs = jnp.maximum((have + GANG - 1) // GANG, 1)
            spare = spot[q]

            def gang(g, carry):
                left = have - g * GANG
                for j in range(GANG):
                    key = slots[row * ROOM + g * GANG + j]
                    plan[(total + g) * WIDTH + j] = jnp.where(j < left, key, spare)
                plan[(total + g) * WIDTH + GANG] = q
                plan[(total + g) * WIDTH + GANG + 1] = left
                plan[(total + g) * WIDTH + GANG + 2] = (g == 0).astype(jnp.int32)
                return carry

            lax.fori_loop(0, gangs, gang, 0)
            return total + gangs

        plan[GANGS * WIDTH] = lax.fori_loop(0, OWN, cut, 0)


def pair_lists(code, spot):
    smem = pl.BlockSpec(memory_space=pltpu.SMEM)
    return pl.pallas_call(
        list_kernel,
        in_specs=[smem, smem],
        out_specs=[smem] * 2,
        out_shape=[jax.ShapeDtypeStruct((GANGS * WIDTH + WIDTH,), jnp.int32)] * 2,
        scratch_shapes=[
            pltpu.SMEM((2 * OWN * ROOM + code.shape[0] + WIDTH,), jnp.int32),
            pltpu.SMEM((2 * OWN + 1,), jnp.int32),
        ],
        cost_estimate=pl.CostEstimate(flops=0, bytes_accessed=60_000_000, transcendentals=0),
    )(code, spot)


def attend_kernel(plan, q, kv, o, level, kbuf, vbuf, expo, acc, peak, keep, sums, total, sem):
    gangs = plan[GANGS * WIDTH]
    acc[...] = jnp.zeros_like(acc)
    total[...] = jnp.zeros_like(total)
    peak[...] = jnp.full_like(peak, LOW)

    def copies(t):
        at = lax.rem(t, DEPTH)
        base = jnp.minimum(t, gangs - 1) * WIDTH
        made = []
        for j in range(GANG):
            key = plan[base + j]
            part = pl.ds(j * BLOCK, BLOCK)
            made.append(
                pltpu.make_async_copy(
                    kv.at[key, pl.ds(0, BLOCK)], kbuf.at[at, part], sem.at[at, 0, j]
                )
            )
            made.append(
                pltpu.make_async_copy(
                    kv.at[key, pl.ds(BLOCK, HD)], vbuf.at[at, :, part], sem.at[at, 1, j]
                )
            )
        return made

    def fetch(t):
        for copy in copies(t):
            copy.start()

    def wait(t):
        for copy in copies(t):
            copy.wait()

    def weigh(t):
        at, side = lax.rem(t, DEPTH), lax.rem(t, 2)
        base = jnp.minimum(t, gangs - 1) * WIDTH
        row, left, first = plan[base + GANG], plan[base + GANG + 1], plan[base + GANG + 2]
        scores = lax.dot_general(
            kbuf[at], q[row], (((1,), (1,)), ((), ())), preferred_element_type=jnp.float32
        )
        parts = []
        for j in range(GANG):
            bias = jnp.where(j < left, 0.0, LOW)
            parts.append(scores[j * BLOCK : (j + 1) * BLOCK] * SCALE + bias)
        most = parts[0]
        for part in parts[1:]:
            most = jnp.maximum(most, part)
        old = jnp.where(first == 1, LOW, peak[1 - side, 0:1])
        new = jnp.maximum(old, jnp.max(most, axis=0, keepdims=True))
        summed = None
        for j, part in enumerate(parts):
            raised = jnp.exp2(part - new)
            expo[side, pl.ds(j * BLOCK, BLOCK)] = raised.astype(jnp.bfloat16)
            summed = raised if summed is None else summed + raised
        peak[side, 0:1] = new
        keep[side, 0:1] = jnp.exp2(old - new)
        sums[side, 0:1] = jnp.sum(summed, axis=0, keepdims=True)

    def mix(t):
        at, side = lax.rem(t, DEPTH), lax.rem(t, 2)
        row = plan[t * WIDTH + GANG]
        mixed = jnp.dot(vbuf[at], expo[side], preferred_element_type=jnp.float32)
        kept = keep[side, 0:1]
        whole = total[0:1] * kept + sums[side, 0:1]
        value = acc[...] * kept + mixed
        total[0:1] = whole
        acc[...] = value
        o[row] = (value * (1.0 / whole)).astype(o.dtype)
        level[row] = peak[side, 0:1] + jnp.log2(whole)

    for t in range(DEPTH - 2):
        fetch(t)
    wait(0)
    weigh(0)

    def step(t, carry):
        fetch(t + DEPTH - 2)
        wait(t + 1)
        mix(t)
        weigh(t + 1)
        return carry

    lax.fori_loop(0, gangs, step, 0)
    for extra in range(1, DEPTH - 2):
        wait(gangs + extra)


def attend(plan, q, kv, kind):
    anywhere = pl.BlockSpec(memory_space=pl.ANY)
    row = pltpu.VMEM((2, 8, BLOCK), jnp.float32)
    return pl.pallas_call(
        attend_kernel,
        grid_spec=pltpu.PrefetchScalarGridSpec(
            num_scalar_prefetch=1,
            grid=(1,),
            in_specs=[pl.BlockSpec((OWN, BLOCK, HD), lambda i, *_: (0, 0, 0)), anywhere],
            out_specs=[
                pl.BlockSpec((OWN, HD, BLOCK), lambda i, *_: (0, 0, 0)),
                pl.BlockSpec((OWN, 1, BLOCK), lambda i, *_: (0, 0, 0)),
            ],
            scratch_shapes=[
                pltpu.VMEM((DEPTH, GANG * BLOCK, HD), jnp.bfloat16),
                pltpu.VMEM((DEPTH, HD, GANG * BLOCK), jnp.bfloat16),
                pltpu.VMEM((2, GANG * BLOCK, BLOCK), jnp.bfloat16),
                pltpu.VMEM((HD, BLOCK), jnp.float32),
                row,
                row,
                row,
                pltpu.VMEM((8, BLOCK), jnp.float32),
                pltpu.SemaphoreType.DMA((DEPTH, 2, GANG)),
            ],
        ),
        out_shape=[
            jax.ShapeDtypeStruct((OWN, HD, BLOCK), kind),
            jax.ShapeDtypeStruct((OWN, 1, BLOCK), jnp.float32),
        ],
        compiler_params=pltpu.CompilerParams(vmem_limit_bytes=50 << 20),
        cost_estimate=pl.CostEstimate(
            flops=100 * 4 * BLOCK**3, bytes_accessed=40 << 20, transcendentals=100 * BLOCK**2
        ),
    )(plan, q, kv)


def combine_kernel(mine, my_level, other, other_level, o):
    for q in range(OWN):
        a, b = my_level[q], other_level[q]
        top = jnp.maximum(a, b)
        share_a, share_b = jnp.exp2(a - top), jnp.exp2(b - top)
        scale = 1.0 / (share_a + share_b)
        value = mine[q] * (share_a * scale) + other[q].astype(jnp.float32) * (share_b * scale)
        o[q] = value.T.astype(o.dtype)


def combine(*parts):
    return pl.pallas_call(
        combine_kernel,
        out_shape=jax.ShapeDtypeStruct((OWN, BLOCK, HD), jnp.bfloat16),
        compiler_params=pltpu.CompilerParams(vmem_limit_bytes=32 << 20),
        cost_estimate=pl.CostEstimate(flops=0, bytes_accessed=8 << 20, transcendentals=0),
    )(*parts)


def pack_kernel(keys, values, o):
    for n in range(o.shape[0]):
        part = pl.ds(n * HD, HD)
        o[n, pl.ds(0, BLOCK)] = keys[:, part]
        o[n, pl.ds(BLOCK, HD)] = values[:, part].T


def pack(keys, values):
    heads, step = keys.shape[1] // HD, 8
    rows = pl.BlockSpec((BLOCK, step * HD), lambda i: (0, i))
    return pl.pallas_call(
        pack_kernel,
        grid=(heads // step,),
        in_specs=[rows, rows],
        out_specs=pl.BlockSpec((step, BLOCK + HD, HD), lambda i: (i, 0, 0)),
        out_shape=jax.ShapeDtypeStruct((heads, BLOCK + HD, HD), keys.dtype),
        cost_estimate=pl.CostEstimate(flops=0, bytes_accessed=4 << 20, transcendentals=0),
    )(keys, values)


def place_of(block):
    ctx, rest = block // 32, block % 32
    pair, rank, split = (jnp.zeros_like(block) for _ in range(3))
    for i, axis in enumerate(AXES):
        bit = (rest >> (len(AXES) - 1 - i)) & 1
        if axis == SPLIT:
            split = bit
        elif axis == PAIR:
            pair = bit
        else:
            rank = rank * 2 + bit
    return pair, rank, ctx * 2 + split


def pair_codes(pattern, my_pair, my_rank):
    key_pair, key_rank, key_slot = place_of(jnp.arange(pattern.shape[0], dtype=jnp.int32))
    pair, rank, slot = place_of(pattern)
    here = (key_pair[:, None] == my_pair) & (rank == my_rank)
    code = jnp.where(here, slot + OWN * (pair == my_pair), 2 * OWN)
    spot = jnp.concatenate(
        [my_rank * OWN + jnp.arange(OWN, dtype=jnp.int32), key_rank * OWN + key_slot]
    )
    return code.reshape(-1).astype(jnp.int32), spot


def body(queries, keys, values, pattern):
    exchange = ("ctx", SPLIT)
    heads = keys.shape[1] // HD

    def regroup(x):
        return lax.all_to_all(x, exchange, split_axis=0, concat_axis=0, tiled=True)

    def swap(x):
        return lax.ppermute(x, PAIR, [(0, 1), (1, 0)])

    my_rank = jnp.int32(0)
    for axis in GROUP:
        my_rank = my_rank * 2 + lax.axis_index(axis)
    plans = pair_lists(*pair_codes(pattern, lax.axis_index(PAIR), my_rank))

    split = (BLOCK, heads, HD)
    both = regroup(pack(keys, values))
    both, queries = lax.optimization_barrier((both, queries))
    gathered = lax.all_gather(both, GROUP, axis=0, tiled=True)
    mine = regroup(jnp.transpose(queries.reshape(split), (1, 0, 2)))
    other = swap(mine)
    for_other, other_level = attend(plans[0], other, gathered, jnp.bfloat16)
    from_other, from_level = swap(for_other), swap(other_level)
    own, own_level = attend(plans[1], mine, gathered, jnp.float32)
    out = regroup(combine(own, own_level, from_other, from_level))
    return jnp.transpose(out, (1, 0, 2)).reshape(queries.shape)


def solution(mesh):
    fine = Mesh(mesh.devices.reshape(2, 2, 2, 2, 2, 16), AXES + ("ctx",))
    rows = P(("ctx",) + AXES, None)
    return jax.shard_map(
        body, mesh=fine, in_specs=(rows, rows, rows, P()), out_specs=rows, check_vma=False
    )
```

time: 407 us -> 339 us (0.83)
  waiting for transfers between devices: 122 us -> 4.28 us
  blocking collectives: 200 us -> 246 us
  Pallas kernels: 49.5 us -> 58.4 us
  local copies, waits for them, and re-layouts: 13 us -> 6.19 us
    all_gather x2 -> x1, waiting for transfers between devices: 88.7 us -> 0.01 us  [body(): gathered = lax.all_gather(both, GROUP, axis=0, tiled=True)]
    all_to_all x3, blocking collectives: 200 us -> 246 us  [regroup(): return lax.all_to_all(x, exchange, split_axis=0, concat_axis=0, tiled=True)]
    all_to_all x1 -> x0, waiting for transfers between devices: 33.4 us -> none  [to_heads(): return lax.all_to_all(x, exchange, split_axis=1, concat_axis=0, tiled=True)]
    ppermute x0 -> x3, starting transfers between devices: none -> 7.58 us  [swap(): return lax.ppermute(x, PAIR, [(0, 1), (1, 0)])]
    all_to_all x1 -> x0, starting transfers between devices: 7.03 us -> none  [to_heads(): return lax.all_to_all(x, exchange, split_axis=1, concat_axis=0, tiled=True)]
    pallas_call x1 -> x3, Pallas kernels: 18.1 us -> 23.4 us  [the longest x1 18.9 us: pair_lists(): pl.pallas_call(list_kernel, in_specs=[smem, smem], out_specs=[smem] * 2,...]
    all_to_all x5 -> x0, local copies, waits for them, and re-layouts: 4.6 us -> none  [the longest x3 2.63 us: to_heads(): return lax.all_to_all(x, exchange, split_axis=1, concat_axis=0, tiled=True)]
    ppermute x0 -> x3, waiting for transfers between devices: none -> 4.26 us  [swap(): return lax.ppermute(x, PAIR, [(0, 1), (1, 0)])]
  transfers between devices with their start and end apart: 3 -> 4, of which waited for: 2 -> 2; matrix products, arithmetic and copies ran while one was open for 2% -> 1% of each run, Pallas kernels for 4% -> 11%
where the time goes in v2:
time: 339 us; the launch traced here: 337 us
  blocking collectives  246 us (73%)
  Pallas kernels  58.4 us (17%)
  between operations  13.5 us (4%)
  starting transfers between devices  7.58 us (2%)
  local copies, waits for them, and re-layouts  6.19 us (2%)
  waiting for transfers between devices  4.28 us (1%)
    all_to_all x3, blocking collectives, regroup(): return lax.all_to_all(x, exchange, split_axis=0, concat_axis=0, tiled=True)  246 us
    pallas_call x2, Pallas kernels, attend(): pl.pallas_call(attend_kernel, grid_spec=pltpu.PrefetchScalarGridSpec(num_...  35 us
    pallas_call x1, Pallas kernels, pair_lists(): pl.pallas_call(list_kernel, in_specs=[smem, smem], out_specs=[smem] * 2,...  18.9 us
    ppermute x3, starting transfers between devices, swap(): return lax.ppermute(x, PAIR, [(0, 1), (1, 0)])  7.58 us
  transfers between devices with their start and end apart: 4, of which 2 were waited for; matrix products, arithmetic and copies ran while one was open for 1% of the time, Pallas kernels for 11%

profile of v2, /device:TPU:1, one launch (start us, length us, event | category | flops | bytes accessed | tf_op | source)
XLA Modules:
  0.0 336.7 jit_solution(2731342268007097593)
XLA Ops:
  6.5 0.0 all-gather.2.cloned.1.call-start
  6.5 4.0 %shard_map.47 = bf16[32,256,128]{2,1,0:T(8,128)(2,1)} custom-call(bf16[128,4096]{1,0:T(8,128)(2,1)} %keys.1, bf16[128,4096]{1,0:T(8,128)(2,1)} %values.1), custom_call_target="tpu_custom_call" | custom-call | bytes 4194304 | tf_op jit(solution)/shard_map/pallas_call | solution.py:238
  10.5 116.8 %all_to_all.15 = bf16[32,256,128]{2,1,0:T(8,128)(2,1)} all-to-all(bf16[32,256,128]{2,1,0:T(8,128)(2,1)} %shard_map.47), channel_id=1, replica_groups=mesh['yh'=2,'yl'=2,'xh'=2,'xl'=2,'core'=2,'ctx'=16] {'ctx','yh'}, dimensions={0} | all-to-all | bytes 4194304 | tf_op jit(solution)/shard_map/all_to_all | solution.py:278
  127.3 0.0 copy-start.2
  127.3 0.0 all-gather.2.cloned.1.call-update
  127.4 1.2 copy-done.2
  128.6 0.7 copy.11
  129.2 0.0 copy-start.3
  129.2 0.7 copy.12
  129.9 59.9 %all_to_all.16.q = bf16[32,128,128]{2,1,0:T(8,128)(2,1)S(1)} all-to-all(bf16[32,128,128]{2,1,0:T(8,128)(2,1)S(1)} %bitcast.4), channel_id=1, replica_groups=mesh['yh'=2,'yl'=2,'xh'=2,'xl'=2,'core'=2,'ctx'=16] {'ctx','yh'}, dimensions={0} | all-to-all | bytes 2097152 | tf_op jit(solution)/shard_map/all_to_all | solution.py:278
  189.8 2.3 collective-permute-start
  192.1 0.0 copy-done.3
  192.2 0.1 copy.10
  192.4 0.8 reshape.22.code
  193.2 0.7 pad_add_fusion.spot
  193.8 18.9 %shard_map.46 = (s32[5448]{0:T(1024)}, s32[5448]{0:T(1024)}) custom-call(s32[2560]{0:T(1024)} %reshape.22.code, s32[544]{0:T(1024)} %pad_add_fusion.spot), custom_call_target="tpu_custom_call" | custom-call | bytes 60000000 | tf_op jit(solution)/shard_map/pallas_call | solution.py:73
  212.8 1.7 collective-permute-done.q
  214.5 0.0 all-gather.2.cloned.1.call-done.kv
  214.5 0.0 copy-start.1
  214.5 0.7 copy-done.1
  215.2 0.0 copy-start
  215.2 17.2 %shard_map.49 = (bf16[32,128,128]{2,1,0:T(8,128)(2,1)S(1)}, f32[32,1,128]{2,1,0:T(1,128)S(1)}) custom-call(s32[5448]{0:T(1024)S(1)} %copy-done.1, bf16[32,128,128]{2,1,0:T(8,128)(2,1)S(1)} %collective-permute-done.q, bf16[256,256,128]{2,1,0:T(8,128)(2,1)} %all-gather.2.cloned.1.call-done.kv), custom_call_target="tpu_custom_call" | custom-call | flops 838860800 | bytes 41943040 | tf_op jit(solution)/shard_map/pallas_call | solution.py:176
  232.5 2.7 collective-permute-start.1
  235.2 2.5 collective-permute-start.2
  237.8 0.0 copy-done
  237.8 17.8 %shard_map.48 = (f32[32,128,128]{2,1,0:T(8,128)S(1)}, f32[32,1,128]{2,1,0:T(1,128)S(1)}) custom-call(s32[5448]{0:T(1024)S(1)} %copy-done, bf16[32,128,128]{2,1,0:T(8,128)(2,1)S(1)} %all_to_all.16.q, bf16[256,256,128]{2,1,0:T(8,128)(2,1)} %all-gather.2.cloned.1.call-done.kv), custom_call_target="tpu_custom_call" | custom-call | flops 838860800 | bytes 41943040 | tf_op jit(solution)/shard_map/pallas_call | solution.py:176
  255.6 2.5 collective-permute-done.2.other_level
  258.1 0.0 collective-permute-done.1.other
  258.1 0.6 shard_map.50
  258.7 69.2 %all_to_all.17 = bf16[32,128,128]{2,1,0:T(8,128)(2,1)S(1)} all-to-all(bf16[32,128,128]{2,1,0:T(8,128)(2,1)S(1)} %shard_map.50), channel_id=1, replica_groups=mesh['yh'=2,'yl'=2,'xh'=2,'xl'=2,'core'=2,'ctx'=16] {'ctx','yh'}, dimensions={0} | all-to-all | bytes 2097152 | tf_op jit(solution)/shard_map/all_to_all | solution.py:278
  327.9 0.7 copy.13
  328.5 1.3 copy.14
  (4 shorter events, 0.1 us)
Async XLA Ops:
  6.5 208.0 %all-gather.2.cloned.1.call-start = ((), (), s32[]{:S(2)}) async-start(), calls=%async_computation.3 | async-start | bytes 18874368 | tf_op jit(solution)/shard_map/all_gather | solution.py:291
  127.3 1.2 copy-start.2
  129.2 62.9 %copy-start.3 = (s32[512,5]{0,1:T(8,128)S(1)}, s32[512,5]{0,1:T(8,128)}, u32[]{:S(2)}) copy-start(s32[512,5]{0,1:T(8,128)} %param.7) | copy-start | bytes 30724
  189.8 24.7 %collective-permute-start = (bf16[32,128,128]{2,1,0:T(8,128)(2,1)S(1)}, bf16[32,128,128]{2,1,0:T(8,128)(2,1)S(1)}, u32[]{:S(2)}, u32[]{:S(2)}) collective-permute-start(bf16[32,128,128]{2,1,0:T(8,128)(2,1)S(1)} %all_to_all.16.q), channel_id=1, source_target_pairs={{0,128},{128,0},{1,129},{129,1},{2,130},{130,2},{3,131},{131,3},{4... | collective-permute-start | bytes 3145736 | tf_op jit(solution)/shard_map/ppermute | solution.py:281
  214.5 0.7 copy-start.1
  215.2 22.5 %copy-start = (s32[5448]{0:T(1024)S(1)}, s32[5448]{0:T(1024)}, u32[]{:S(2)}) copy-start(s32[5448]{0:T(1024)} %get-tuple-element.13.plan) | copy-start | bytes 65380
  232.5 25.6 %collective-permute-start.1 = (bf16[32,128,128]{2,1,0:T(8,128)(2,1)S(1)}, bf16[32,128,128]{2,1,0:T(8,128)(2,1)S(1)}, u32[]{:S(2)}, u32[]{:S(2)}) collective-permute-start(bf16[32,128,128]{2,1,0:T(8,128)(2,1)S(1)} %get-tuple-element.19), channel_id=1, source_target_pairs={{0,128},{128,0},{1,129},{129,1},{2,130},{130,2},{3,131},{131,3},{4... | collective-permute-start | bytes 3145736 | tf_op jit(solution)/shard_map/ppermute | solution.py:281
  235.2 22.9 %collective-permute-start.2 = (f32[32,1,128]{2,1,0:T(1,128)S(1)}, f32[32,1,128]{2,1,0:T(1,128)S(1)}, u32[]{:S(2)}, u32[]{:S(2)}) collective-permute-start(f32[32,1,128]{2,1,0:T(1,128)S(1)} %get-tuple-element.20), channel_id=1, source_target_pairs={{0,128},{128,0},{1,129},{129,1},{2,130},{130,2},{3,131},{131,3},{4... | collective-permute-start | bytes 49160 | tf_op jit(solution)/shard_map/ppermute | solution.py:281
Sparse Core Ops, SparseCore 0:
  127.5 86.8 all-gather.1
